TPU v7x, 256 devices: a whole 4x4x8 slice. The times are simulated.
256 devices in a mesh: ri: 8 (over y, core), mu: 4 (over x), nu: 8 (over z).
Axes of the slice: x: 4, y: 4, z: 8, core: 2. Of those that a mesh axis runs over, the one named last changes fastest.
Arguments:
- three_center: bfloat16 [32, 2304, 128, 128], P('ri', ('mu', 'nu')), may hold values from -0.15625 to 0.15625
- block_pairs: int32 [2304, 2], P(('mu', 'nu')), may hold values from -1 to 95, as said below
- occ_factor: bfloat16 [12288, 128], P(('mu', 'nu')), may hold values from -6 to 6
- virt_density: bfloat16 [12288, 12288], P(('mu', 'nu'), 'ri'), may hold values from -0.0546875 to 0.0546875
- block_sizes: int32 [96], replicated, may hold values from 96 to 128
- occ_mask: int32 [96], replicated, may hold values 0 or 1
- virt_mask: int32 [96, 96], replicated, may hold values 0 or 1
Outputs:
- transformed: bfloat16 [32, 12288, 128], P('ri', ('mu', 'nu'))
Inputs may be any that keep to these rules, and one draw needn't show every extreme that they name: `block_pairs`: slots k in [d * 72, (d + 1) * 72) belong to device d of mu+nu; a live slot holds a mu block of that device's mu range (the range of 24 blocks of its mu index) and any nu block; empty slots hold -1 in both columns, and the live slots of a device come first. Every mu block appears in exactly 12 live slots, with distinct nu blocks. A device holds at most 72 live slots, and in every mu range some device holds exactly 72.
All inputs are finite; a program needn't handle non-finite values.
Results may differ from a plain program's by a relative error of at most 0.015.
Values may be sent and summed in bfloat16 or wider, within the bound.
A program may use at most 128 MiB of HBM per device.

v0:
```python
import jax
import jax.numpy as jnp
from jax import lax
from jax.sharding import PartitionSpec as P

BS = 128
NB = 96


def body(three_center, block_pairs, occ_factor, virt_density, block_sizes, occ_mask, virt_mask):
    rows_dev = virt_density.shape[0]
    occ_cols = occ_factor.shape[1]
    ri_rows = three_center.shape[0]
    blocks_mu = NB // lax.axis_size("mu")
    total_rows = NB * BS
    inside = jnp.arange(BS, dtype=jnp.int32)[None, :] < block_sizes[:, None]
    keep_occ = (inside & (occ_mask[:, None] > 0)).reshape(total_rows)
    gathered_occ = lax.all_gather(occ_factor, ("mu", "nu"), axis=0, tiled=True)
    occ_kept = jnp.where(keep_occ[:, None], gathered_occ, jnp.zeros((), jnp.bfloat16))
    mu_block = block_pairs[:, 0]
    nu_block = jnp.clip(block_pairs[:, 1], 0, NB - 1)
    slot_live = mu_block >= 0
    occ_blocks = occ_kept.reshape(NB, BS, occ_cols)[nu_block]
    products = jnp.einsum(
        "pkab,kbo->pkao", three_center, occ_blocks, preferred_element_type=jnp.float32
    )
    local_block = mu_block - lax.axis_index("mu") * blocks_mu
    segment_ids = jnp.where(slot_live, local_block, blocks_mu)

    def slot_sum(slab_products):
        return jax.ops.segment_sum(slab_products, segment_ids, num_segments=blocks_mu + 1)[
            :blocks_mu
        ]

    partial_value = jax.vmap(slot_sum)(products)
    partial_value = partial_value.reshape(ri_rows, blocks_mu * BS, occ_cols)
    virt_all = lax.all_gather(virt_density, "ri", axis=1, tiled=True)
    row_start = (lax.axis_index("mu") * lax.axis_size("nu") + lax.axis_index("nu")) * rows_dev
    row_ids = row_start + jnp.arange(rows_dev, dtype=jnp.int32)
    block_pick = (row_ids[:, None] // BS == jnp.arange(NB, dtype=jnp.int32)[None, :]).astype(
        jnp.float32
    )
    mask_rows = jnp.dot(block_pick, virt_mask.astype(jnp.float32)) > 0.5
    row_inside = lax.dynamic_slice_in_dim(inside.reshape(total_rows), row_start, rows_dev)
    keep_virt = (mask_rows[:, :, None] & inside[None, :, :] & row_inside[:, None, None]).reshape(
        rows_dev, total_rows
    )
    virt_kept = jnp.where(keep_virt, virt_all, jnp.zeros((), jnp.bfloat16))
    summed = lax.psum_scatter(
        partial_value.astype(jnp.bfloat16), "nu", scatter_dimension=1, tiled=True
    )
    result = jnp.einsum(
        "sm,pmo->pso",
        virt_kept,
        lax.all_gather(summed, ("mu", "nu"), axis=1, tiled=True),
        preferred_element_type=jnp.float32,
    )
    return result.astype(jnp.bfloat16)


def solution(mesh):
    in_specs = (
        P("ri", ("mu", "nu"), None, None),
        P(("mu", "nu"), None),
        P(("mu", "nu"), None),
        P(("mu", "nu"), "ri"),
        P(),
        P(),
        P(),
    )
    out_specs = P("ri", ("mu", "nu"), None)
    return jax.shard_map(body, mesh=mesh, in_specs=in_specs, out_specs=out_specs, check_vma=False)
```

profile of v0, /device:TPU:8, one launch (start us, length us, event | category | flops | bytes accessed | tf_op | source)
XLA Modules:
  0.0 418.7 jit_solution(11618415687132992076)
XLA Ops:
  7.4 0.0 all-gather.4.cloned.1.call-start
  7.4 0.7 all-gather.4.cloned.1.call-update
  8.1 0.0 reduce-scatter.4.cloned.1.call-start
  8.1 0.8 fusion.26
  8.9 0.7 broadcast_compare_fusion
  9.6 0.7 bitcast_compare_fusion
  10.3 83.2 %all-gather.4.cloned.1.call-done = bf16[12288,128]{1,0:T(8,128)(2,1)} async-done(((bf16[384,128]{1,0:T(8,128)(2,1)}), bf16[12288,128]{1,0:T(8,128)(2,1)}) %all-gather.4.cloned.1.call-update) | async-done | bytes 3145744 | tf_op jit(solution)/shard_map/all_gather | solution.py:18
  93.5 8.4 %broadcast_select_fusion = bf16[12288,128]{1,0:T(8,128)(2,1)S(1)} fusion(bf16[12288,128]{1,0:T(8,128)(2,1)} %all-gather.4.cloned.1.call-done, pred[12288]{0:T(1024)(128)(4,1)S(1)} %get-tuple-element.8), kind=kLoop, calls=%fused_computation.15 | loop fusion | flops 1572864 | bytes 6303744 | tf_op jit(solution)/shard_map/jit(_where)/select_n | solution.py:19
  102.0 2.4 gather_fusion
  104.4 13.5 %fusion.9 = f32[72,4,128,128]{2,3,1,0:T(8,128)} fusion(bf16[4,72,128,128]{3,2,1,0:T(8,128)(2,1)} %param.7, bf16[72,128,128]{2,1,0:T(8,128)(2,1)} %gather_fusion), kind=kOutput, calls=%fused_computation.11 | convolution fusion | flops 1207959552 | bytes 30670848 | tf_op jit(solution)/shard_map/pkab,kbo->pkao/dot_general | solution.py:24
  117.9 18.6 %copy.19 = f32[72,4,128,128]{3,2,1,0:T(8,128)} copy(f32[72,4,128,128]{2,3,1,0:T(8,128)} %fusion.9) | data formatting | bytes 37748736 | tf_op jit(solution)/shard_map/pkab,kbo->pkao/transpose | solution.py:24
  136.5 3.5 broadcast_in_dim.21
  140.1 41.2 %scatter_fusion = f32[4,25,128,128]{3,2,1,0:T(8,128)} fusion(f32[4,25,128,128]{3,2,1,0:T(8,128)} %broadcast_in_dim.21, s32[72]{0:T(128)S(1)} %get-tuple-element.6, f32[72,4,128,128]{3,2,1,0:T(8,128)} %copy.19), kind=kCustom, calls=%fused_computation.1 | custom fusion | flops 4718592 | bytes 56623392 | tf_op jit(solution)/shard_map/vmap()/scatter-add | solution.py:31
  181.3 3.5 slice.19
  184.8 15.0 %copy.26 = bf16[4,3072,128]{2,0,1:T(4,128)(2,1)S(1)} copy(bf16[4,3072,128]{2,1,0:T(8,128)(2,1)S(1)} %bitcast.57) | data formatting | bytes 6291456
  199.8 2.2 copy.44
  202.0 0.0 copy-start.1
  202.0 0.0 copy-start
  202.0 0.0 reduce-scatter.4.cloned.1.call-update
  202.0 0.0 all-gather.8.cloned.1.call-start
  202.1 0.5 all-gather.8.cloned.1.call-update
  202.6 0.2 all-gather.6.cloned.1.call-start
  202.9 43.4 %reduce-scatter.4.cloned.1.call-done = bf16[384,512]{1,0:T(8,128)(2,1)} async-done(((bf16[3072,512]{1,0:T(8,128)(2,1)}), bf16[384,512]{1,0:T(8,128)(2,1)}) %reduce-scatter.4.cloned.1.call-update) | async-done | bytes 393232
  246.2 1.1 reshape.109
  247.3 1.0 copy.27
  248.3 0.0 all-gather.6.cloned.1.call-update
  248.4 0.0 copy-done.1
  248.4 0.3 convolution_compare_fusion
  248.6 0.2 copy.21
  248.8 0.1 dynamic_slice.3
  248.9 0.0 copy-done
  248.9 0.2 lt.49
  249.1 8.2 %all-gather.8.cloned.1.call-done = bf16[384,12288]{1,0:T(8,128)(2,1)} async-done(((bf16[384,1536]{1,0:T(8,128)(2,1)}), bf16[384,12288]{1,0:T(8,128)(2,1)}) %all-gather.8.cloned.1.call-update) | async-done | bytes 9437200 | tf_op jit(solution)/shard_map/all_gather | solution.py:37
  257.3 129.7 %all-gather.6.cloned.1.call-done = bf16[4,12288,128]{1,2,0:T(8,128)(2,1)} async-done(((bf16[4,384,128]{1,2,0:T(8,128)(2,1)}), bf16[4,12288,128]{1,2,0:T(8,128)(2,1)}) %all-gather.6.cloned.1.call-update) | async-done | bytes 12582928 | tf_op jit(solution)/shard_map/all_gather | solution.py:55
  386.9 6.7 %and.60 = pred[384,96,128]{2,1,0:T(32,128)(4,1)S(1)} broadcast(pred[384,96]{1,0:T(8,128)(4,1)S(1)} %copy.21), dimensions={0,1} | broadcast | bytes 4755456 | tf_op jit(solution)/shard_map/and | solution.py:45
  393.6 16.7 %fusion.17 = bf16[4,384,128]{1,2,0:T(8,128)(2,1)S(1)} fusion(bf16[4,12288,128]{1,2,0:T(8,128)(2,1)} %all-gather.6.cloned.1.call-done, bf16[384,12288]{1,0:T(8,128)(2,1)} %all-gather.8.cloned.1.call-done, pred[48,8,96,128]{3,2,1,0:T(32,128)(4,1)S(1)} %bitcast.60, pred[384]{0:T(512)(128)(4,1)S(1)} %dynamic_slice.3, pred[12288]{0:T(1024)(128)(4,1)S(1)} %bitcast_compare_fusion.1), kind=kOutput, calls=%fused_computation.18 | convolution fusion | flops 4846190592 | bytes 27144576 | tf_op jit(solution)/shard_map/sm,pmo->pso/dot_general | solution.py:52
  410.3 0.9 copy.22
  (3 shorter events, 0.0 us)
Async XLA Ops:
  7.4 86.1 %all-gather.4.cloned.1.call-start = ((), (), s32[]{:S(2)}) async-start(), calls=%async_computation.1 | async-start | bytes 3244032 | tf_op jit(solution)/shard_map/all_gather | solution.py:18
  8.1 238.1 %reduce-scatter.4.cloned.1.call-start = ((), (), s32[]{:S(2)}) async-start(), calls=%async_computation.4 | async-start | bytes 3538944
  202.0 46.3 %copy-start.1 = (s32[96,96]{1,0:T(8,128)S(1)}, s32[96,96]{1,0:T(8,128)}, u32[]{:S(2)}) copy-start(s32[96,96]{1,0:T(8,128)} %param.13) | copy-start | bytes 110596
  202.0 46.9 %copy-start = (s32[96]{0:T(128)S(1)}, s32[96]{0:T(128)}, u32[]{:S(2)}) copy-start(s32[96]{0:T(128)} %param.11) | copy-start | bytes 1156
  202.0 55.2 %all-gather.8.cloned.1.call-start = ((), (), s32[]{:S(2)}) async-start(), calls=%async_computation.3 | async-start | bytes 10616832 | tf_op jit(solution)/shard_map/all_gather | solution.py:37
  202.6 184.3 %all-gather.6.cloned.1.call-start = ((), (), s32[]{:S(2)}) async-start(), calls=%async_computation.2 | async-start | bytes 12976128 | tf_op jit(solution)/shard_map/all_gather | solution.py:55
Sparse Core Ops, SparseCore 0:
  10.8 82.6 all-gather.3
  202.2 43.9 reduce-scatter.3
Sparse Core Ops, SparseCore 1:
  204.4 52.9 all-gather.7
  259.6 127.2 all-gather.5
where the time goes:
time: 419 us
  waiting for transfers between devices  266 us (63%)
  local copies, waits for them, and re-layouts  55.4 us (13%)
  other arithmetic  51.9 us (12%)
  matrix products  30.5 us (7%)
  between operations  15 us (4%)
    all_gather x1, waiting for transfers between devices, body(): lax.all_gather(summed, ('mu', 'nu'), axis=1, tiled=True)  130 us
    all_gather x1, waiting for transfers between devices, body(): gathered_occ = lax.all_gather(occ_factor, ('mu', 'nu'), axis=0, tiled=True)  83.2 us
    unnamed x5, waiting for transfers between devices  44.6 us
    scatter-add x1, other arithmetic, slot_sum(): jax.ops.segment_sum(slab_products, segment_ids, num_segments=blocks_mu + 1)  41.2 us
    unnamed x8, local copies, waits for them, and re-layouts  19.3 us
    transpose x1, local copies, waits for them, and re-layouts, body(): jnp.einsum('pkab,kbo->pkao', three_center, occ_blocks, preferred_element_...  18.6 us
    dot_general x1, matrix products, body(): jnp.einsum('sm,pmo->pso', virt_kept, lax.all_gather(summed, ('mu', 'nu'),...  16.7 us
    dot_general x1, matrix products, body(): jnp.einsum('pkab,kbo->pkao', three_center, occ_blocks, preferred_element_...  13.5 us
  transfers between devices with their start and end apart: 4, of which 4 were waited for; matrix products, arithmetic and copies ran while one was open for 1% of the time, Pallas kernels for 0%

commit v1 on v0

--- a/solution.py
+++ b/solution.py
@@ -34,7 +34,12 @@
 
     partial_value = jax.vmap(slot_sum)(products)
     partial_value = partial_value.reshape(ri_rows, blocks_mu * BS, occ_cols)
-    virt_all = lax.all_gather(virt_density, "ri", axis=1, tiled=True)
+    ring = [virt_density]
+    for hop in range(7):
+        ring.append(lax.ppermute(ring[-1], "ri", [(dev, (dev + 1) % 8) for dev in range(8)]))
+    virt_all = jnp.roll(
+        jnp.concatenate(ring[::-1], axis=1), (lax.axis_index("ri") + 1) * ring[0].shape[1], axis=1
+    )
     row_start = (lax.axis_index("mu") * lax.axis_size("nu") + lax.axis_index("nu")) * rows_dev
     row_ids = row_start + jnp.arange(rows_dev, dtype=jnp.int32)
     block_pick = (row_ids[:, None] // BS == jnp.arange(NB, dtype=jnp.int32)[None, :]).astype(

time: 419 us -> 429 us (1.024)
  the two profiles are of different devices: /device:TPU:8 before, /device:TPU:2 now
where the time goes in v1:
time: 429 us; the launch traced here: 428 us
  waiting for transfers between devices  242 us (56%)
  local copies, waits for them, and re-layouts  87.5 us (20%)
  other arithmetic  51.3 us (12%)
  matrix products  33.6 us (8%)
  between operations  13.2 us (3%)
    ppermute x7, waiting for transfers between devices, body(): lax.ppermute(ring[-1], 'ri', [(dev, (dev + 1) % 8) for dev in range(8)])  114 us
    all_gather x1, waiting for transfers between devices, body(): gathered_occ = lax.all_gather(occ_factor, ('mu', 'nu'), axis=0, tiled=True)  82.1 us
    unnamed x37, local copies, waits for them, and re-layouts  47.5 us
    unnamed x4, waiting for transfers between devices  45.6 us
    scatter-add x1, other arithmetic, slot_sum(): jax.ops.segment_sum(slab_products, segment_ids, num_segments=blocks_mu + 1)  40.7 us
    transpose x1, local copies, waits for them, and re-layouts, body(): jnp.einsum('pkab,kbo->pkao', three_center, occ_blocks, preferred_element_...  18.6 us
    dot_general x1, matrix products, body(): jnp.einsum('sm,pmo->pso', virt_kept, lax.all_gather(summed, ('mu', 'nu'),...  18.3 us
    dot_general x1, matrix products, body(): jnp.einsum('pkab,kbo->pkao', three_center, occ_blocks, preferred_element_...  13.5 us
  transfers between devices with their start and end apart: 10, of which 9 were waited for; matrix products, arithmetic and copies ran while one was open for 8% of the time, Pallas kernels for 0%

profile of v1, /device:TPU:2, one launch (start us, length us, event | category | flops | bytes accessed | tf_op | source)
XLA Modules:
  0.0 427.9 jit_solution(5961937905699308010)
XLA Ops:
  6.5 0.7 all-gather.3.cloned.1.call-update
  7.3 0.0 reduce-scatter.4.cloned.1.call-start
  7.3 0.8 fusion.27
  8.1 0.7 broadcast_compare_fusion
  8.7 0.7 bitcast_compare_fusion
  9.5 82.1 %all-gather.3.cloned.1.call-done = bf16[12288,128]{1,0:T(8,128)(2,1)} async-done(((bf16[384,128]{1,0:T(8,128)(2,1)}), bf16[12288,128]{1,0:T(8,128)(2,1)}) %all-gather.3.cloned.1.call-update) | async-done | bytes 3145744 | tf_op jit(solution)/shard_map/all_gather | solution.py:18
  91.6 8.4 %broadcast_select_fusion = bf16[12288,128]{1,0:T(8,128)(2,1)S(1)} fusion(bf16[12288,128]{1,0:T(8,128)(2,1)} %all-gather.3.cloned.1.call-done, pred[12288]{0:T(1024)(128)(4,1)S(1)} %get-tuple-element.8), kind=kLoop, calls=%fused_computation.16 | loop fusion | flops 1572864 | bytes 6303744 | tf_op jit(solution)/shard_map/jit(_where)/select_n | solution.py:19
  100.0 2.5 gather_fusion
  102.5 13.5 %fusion.10 = f32[72,4,128,128]{2,3,1,0:T(8,128)} fusion(bf16[4,72,128,128]{3,2,1,0:T(8,128)(2,1)} %param.7, bf16[72,128,128]{2,1,0:T(8,128)(2,1)} %gather_fusion), kind=kOutput, calls=%fused_computation.12 | convolution fusion | flops 1207959552 | bytes 30670848 | tf_op jit(solution)/shard_map/pkab,kbo->pkao/dot_general | solution.py:24
  116.0 18.6 %copy.19 = f32[72,4,128,128]{3,2,1,0:T(8,128)} copy(f32[72,4,128,128]{2,3,1,0:T(8,128)} %fusion.10) | data formatting | bytes 37748736 | tf_op jit(solution)/shard_map/pkab,kbo->pkao/transpose | solution.py:24
  134.7 3.5 broadcast_in_dim.21
  138.2 40.7 %scatter_fusion = f32[4,25,128,128]{3,2,1,0:T(8,128)} fusion(f32[4,25,128,128]{3,2,1,0:T(8,128)} %broadcast_in_dim.21, s32[72]{0:T(128)S(1)} %get-tuple-element.6, f32[72,4,128,128]{3,2,1,0:T(8,128)} %copy.19), kind=kCustom, calls=%fused_computation.1 | custom fusion | flops 4718592 | bytes 56623392 | tf_op jit(solution)/shard_map/vmap()/scatter-add | solution.py:31
  178.9 3.5 slice.19
  182.4 0.0 copy-start
  182.4 0.0 copy-start.7
  182.4 15.0 %copy.26 = bf16[4,3072,128]{2,0,1:T(4,128)(2,1)S(1)} copy(bf16[4,3072,128]{2,1,0:T(8,128)(2,1)S(1)} %bitcast.57) | data formatting | bytes 6291456
  197.4 2.2 copy.44
  199.6 0.0 reduce-scatter.4.cloned.1.call-update
  199.7 0.2 all-gather.5.cloned.1.call-start
  199.9 44.9 %reduce-scatter.4.cloned.1.call-done = bf16[384,512]{1,0:T(8,128)(2,1)} async-done(((bf16[3072,512]{1,0:T(8,128)(2,1)}), bf16[384,512]{1,0:T(8,128)(2,1)}) %reduce-scatter.4.cloned.1.call-update) | async-done | bytes 393232
  244.7 1.1 reshape.109
  245.8 1.0 copy.27
  246.8 0.0 all-gather.5.cloned.1.call-update
  246.9 0.0 collective-permute-start
  246.9 16.8 %collective-permute-done = bf16[384,1536]{1,0:T(8,128)(2,1)S(1)} collective-permute-done((bf16[384,1536]{1,0:T(8,128)(2,1)S(1)}, bf16[384,1536]{1,0:T(8,128)(2,1)S(1)}, u32[]{:S(2)}, u32[]{:S(2)}) %collective-permute-start) | collective-permute-done | bytes 1179680 | tf_op jit(solution)/shard_map/ppermute | solution.py:39
  263.7 0.0 collective-permute-start.1
  263.7 16.8 %collective-permute-done.1 = bf16[384,1536]{1,0:T(8,128)(2,1)S(1)} collective-permute-done((bf16[384,1536]{1,0:T(8,128)(2,1)S(1)}, bf16[384,1536]{1,0:T(8,128)(2,1)S(1)}, u32[]{:S(2)}, u32[]{:S(2)}) %collective-permute-start.1) | collective-permute-done | bytes 1179680 | tf_op jit(solution)/shard_map/ppermute | solution.py:39
  280.6 0.0 collective-permute-start.2
  280.6 16.8 %collective-permute-done.2 = bf16[384,1536]{1,0:T(8,128)(2,1)S(1)} collective-permute-done((bf16[384,1536]{1,0:T(8,128)(2,1)S(1)}, bf16[384,1536]{1,0:T(8,128)(2,1)S(1)}, u32[]{:S(2)}, u32[]{:S(2)}) %collective-permute-start.2) | collective-permute-done | bytes 1179680 | tf_op jit(solution)/shard_map/ppermute | solution.py:39
  297.4 1.0 copy-done.1
  298.4 0.0 collective-permute-start.3
  298.4 16.8 %collective-permute-done.3 = bf16[384,1536]{1,0:T(8,128)(2,1)S(1)} collective-permute-done((bf16[384,1536]{1,0:T(8,128)(2,1)S(1)}, bf16[384,1536]{1,0:T(8,128)(2,1)S(1)}, u32[]{:S(2)}, u32[]{:S(2)}) %collective-permute-start.3) | collective-permute-done | bytes 1179680 | tf_op jit(solution)/shard_map/ppermute | solution.py:39
  315.3 1.0 copy-done.3
  316.3 0.0 collective-permute-start.4
  316.3 16.8 %collective-permute-done.4 = bf16[384,1536]{1,0:T(8,128)(2,1)S(1)} collective-permute-done((bf16[384,1536]{1,0:T(8,128)(2,1)S(1)}, bf16[384,1536]{1,0:T(8,128)(2,1)S(1)}, u32[]{:S(2)}, u32[]{:S(2)}) %collective-permute-start.4) | collective-permute-done | bytes 1179680 | tf_op jit(solution)/shard_map/ppermute | solution.py:39
  333.2 1.0 copy-done.5
  334.2 0.0 collective-permute-start.5
  334.2 16.9 %collective-permute-done.5 = bf16[384,1536]{1,0:T(8,128)(2,1)} collective-permute-done((bf16[384,1536]{1,0:T(8,128)(2,1)S(1)}, bf16[384,1536]{1,0:T(8,128)(2,1)}, u32[]{:S(2)}, u32[]{:S(2)}) %collective-permute-start.5) | collective-permute-done | bytes 1179680 | tf_op jit(solution)/shard_map/ppermute | solution.py:39
  351.2 0.0 collective-permute-start.6
  351.2 1.7 convolution_compare_fusion
  352.9 1.5 copy.21
  354.4 0.6 dynamic_slice.7
  355.0 0.2 lt.61
  355.1 13.2 %collective-permute-done.6 = bf16[384,1536]{1,0:T(8,128)(2,1)} collective-permute-done((bf16[384,1536]{1,0:T(8,128)(2,1)}, bf16[384,1536]{1,0:T(8,128)(2,1)}, u32[]{:S(2)}, u32[]{:S(2)}) %collective-permute-start.6) | collective-permute-done | bytes 1179680 | tf_op jit(solution)/shard_map/ppermute | solution.py:39
  368.3 2.4 constant_dynamic-update-slice_fusion.15
  370.7 2.4 constant_dynamic-update-slice_fusion.14
  373.1 2.5 constant_dynamic-update-slice_fusion.13
  375.6 2.5 constant_dynamic-update-slice_fusion.12
  378.1 1.1 constant_dynamic-update-slice_fusion.11
  379.3 1.1 constant_dynamic-update-slice_fusion.10
  380.4 1.2 constant_dynamic-update-slice_fusion.9
  381.6 1.1 constant_dynamic-update-slice_fusion.8
  382.7 2.4 constant_dynamic-update-slice_fusion.7
  385.1 2.4 constant_dynamic-update-slice_fusion.6
  387.5 0.0 copy-done.6
  387.5 1.2 constant_dynamic-update-slice_fusion.5
  388.7 1.1 constant_dynamic-update-slice_fusion.4
  389.8 1.1 constant_dynamic-update-slice_fusion.3
  390.9 1.2 constant_dynamic-update-slice_fusion.2
  392.1 1.2 constant_dynamic-update-slice_fusion.1
  393.3 1.1 constant_dynamic-update-slice_fusion
  394.4 7.6 %and.66 = pred[384,96,128]{2,1,0:T(32,128)(4,1)S(1)} broadcast(pred[384,96]{1,0:T(8,128)(4,1)} %copy.21), dimensions={0,1} | broadcast | bytes 4755456 | tf_op jit(solution)/shard_map/and | solution.py:50
  402.1 18.3 %fusion.18 = bf16[4,384,128]{1,2,0:T(8,128)(2,1)S(1)} fusion(bf16[4,12288,128]{1,2,0:T(8,128)(2,1)} %all-gather.5.cloned.1.call-done, pred[48,8,96,128]{3,2,1,0:T(32,128)(4,1)S(1)} %bitcast.60, bf16[384,24576]{1,0:T(8,128)(2,1)} %constant_dynamic-update-slice_fusion, s32[]{:T(128)S(6)} %select_n.49, pred[384]{0:T(512)(128)(4,1)S(1)} %copy-done.8, ...), kind=kOutput, calls=%fused_computation.19 | convolution fusion | flops 4846190592 | bytes 27144580 | tf_op jit(solution)/shard_map/sm,pmo->pso/dot_general | solution.py:57
  420.4 0.9 copy.22
  (17 shorter events, 0.1 us)
Async XLA Ops:
  6.5 85.1 %all-gather.3.cloned.1.call-start = ((), (), s32[]{:S(2)}) async-start(), calls=%async_computation.1 | async-start | bytes 3244032 | tf_op jit(solution)/shard_map/all_gather | solution.py:18
  7.3 237.5 %reduce-scatter.4.cloned.1.call-start = ((), (), s32[]{:S(2)}) async-start(), calls=%async_computation.3 | async-start | bytes 3538944
  182.4 64.5 %copy-start = (bf16[384,1536]{1,0:T(8,128)(2,1)S(1)}, bf16[384,1536]{1,0:T(8,128)(2,1)}, u32[]{:S(2)}) copy-start(bf16[384,1536]{1,0:T(8,128)(2,1)} %param.10) | copy-start | bytes 3538948
  182.4 172.6 %copy-start.7 = (s32[96]{0:T(128)S(1)}, s32[96]{0:T(128)}, u32[]{:S(2)}) copy-start(s32[96]{0:T(128)} %param.11) | copy-start | bytes 1156
  199.7 194.8 %all-gather.5.cloned.1.call-start = ((), (), s32[]{:S(2)}) async-start(), calls=%async_computation.2 | async-start | bytes 12976128 | tf_op jit(solution)/shard_map/all_gather | solution.py:60
  246.9 16.9 %collective-permute-start = (bf16[384,1536]{1,0:T(8,128)(2,1)S(1)}, bf16[384,1536]{1,0:T(8,128)(2,1)S(1)}, u32[]{:S(2)}, u32[]{:S(2)}) collective-permute-start(bf16[384,1536]{1,0:T(8,128)(2,1)S(1)} %copy-done), channel_id=1, source_target_pairs={{0,32},{32,64},{64,96},{96,128},{128,160},{160,192},{192,224},{224... | collective-permute-start | bytes 3538952 | tf_op jit(solution)/shard_map/ppermute | solution.py:39
  263.7 16.8 %collective-permute-start.1 = (bf16[384,1536]{1,0:T(8,128)(2,1)S(1)}, bf16[384,1536]{1,0:T(8,128)(2,1)S(1)}, u32[]{:S(2)}, u32[]{:S(2)}) collective-permute-start(bf16[384,1536]{1,0:T(8,128)(2,1)S(1)} %collective-permute-done), channel_id=1, source_target_pairs={{0,32},{32,64},{64,96},{96,128},{128,160},{160,192},{192,224},{224... | collective-permute-start | bytes 3538952 | tf_op jit(solution)/shard_map/ppermute | solution.py:39
  280.6 16.8 %collective-permute-start.2 = (bf16[384,1536]{1,0:T(8,128)(2,1)S(1)}, bf16[384,1536]{1,0:T(8,128)(2,1)S(1)}, u32[]{:S(2)}, u32[]{:S(2)}) collective-permute-start(bf16[384,1536]{1,0:T(8,128)(2,1)S(1)} %collective-permute-done.1), channel_id=1, source_target_pairs={{0,32},{32,64},{64,96},{96,128},{128,160},{160,192},{192,224},{224... | collective-permute-start | bytes 3538952 | tf_op jit(solution)/shard_map/ppermute | solution.py:39
  297.4 1.0 copy-start.1
  298.4 16.8 %collective-permute-start.3 = (bf16[384,1536]{1,0:T(8,128)(2,1)S(1)}, bf16[384,1536]{1,0:T(8,128)(2,1)S(1)}, u32[]{:S(2)}, u32[]{:S(2)}) collective-permute-start(bf16[384,1536]{1,0:T(8,128)(2,1)S(1)} %collective-permute-done.2), channel_id=1, source_target_pairs={{0,32},{32,64},{64,96},{96,128},{128,160},{160,192},{192,224},{224... | collective-permute-start | bytes 3538952 | tf_op jit(solution)/shard_map/ppermute | solution.py:39
  315.3 1.0 copy-start.3
  316.3 16.8 %collective-permute-start.4 = (bf16[384,1536]{1,0:T(8,128)(2,1)S(1)}, bf16[384,1536]{1,0:T(8,128)(2,1)S(1)}, u32[]{:S(2)}, u32[]{:S(2)}) collective-permute-start(bf16[384,1536]{1,0:T(8,128)(2,1)S(1)} %collective-permute-done.3), channel_id=1, source_target_pairs={{0,32},{32,64},{64,96},{96,128},{128,160},{160,192},{192,224},{224... | collective-permute-start | bytes 3538952 | tf_op jit(solution)/shard_map/ppermute | solution.py:39
  333.2 1.1 copy-start.5
  334.2 16.9 %collective-permute-start.5 = (bf16[384,1536]{1,0:T(8,128)(2,1)S(1)}, bf16[384,1536]{1,0:T(8,128)(2,1)}, u32[]{:S(2)}, u32[]{:S(2)}) collective-permute-start(bf16[384,1536]{1,0:T(8,128)(2,1)S(1)} %collective-permute-done.4), channel_id=1, source_target_pairs={{0,32},{32,64},{64,96},{96,128},{128,160},{160,192},{192,224},{224... | collective-permute-start | bytes 3538952 | tf_op jit(solution)/shard_map/ppermute | solution.py:39
  351.2 17.2 %collective-permute-start.6 = (bf16[384,1536]{1,0:T(8,128)(2,1)}, bf16[384,1536]{1,0:T(8,128)(2,1)}, u32[]{:S(2)}, u32[]{:S(2)}) collective-permute-start(bf16[384,1536]{1,0:T(8,128)(2,1)} %collective-permute-done.5), channel_id=1, source_target_pairs={{0,32},{32,64},{64,96},{96,128},{128,160},{160,192},{192,224},{224... | collective-permute-start | bytes 3538952 | tf_op jit(solution)/shard_map/ppermute | solution.py:39
  354.4 23.7 %copy-start.2 = (bf16[384,1536]{1,0:T(8,128)(2,1)S(1)}, bf16[384,1536]{1,0:T(8,128)(2,1)}, u32[]{:S(2)}) copy-start(bf16[384,1536]{1,0:T(8,128)(2,1)} %copy-done.1) | copy-start | bytes 3538948
  373.1 14.4 %copy-start.6 = (bf16[384,1536]{1,0:T(8,128)(2,1)S(1)}, bf16[384,1536]{1,0:T(8,128)(2,1)}, u32[]{:S(2)}) copy-start(bf16[384,1536]{1,0:T(8,128)(2,1)} %copy-done.5) | copy-start | bytes 3538948
  375.6 13.1 %copy-start.4 = (bf16[384,1536]{1,0:T(8,128)(2,1)S(1)}, bf16[384,1536]{1,0:T(8,128)(2,1)}, u32[]{:S(2)}) copy-start(bf16[384,1536]{1,0:T(8,128)(2,1)} %copy-done.3) | copy-start | bytes 3538948
  387.5 14.5 %copy-start.8 = (pred[384]{0:T(512)(128)(4,1)S(1)}, pred[384]{0:T(512)(128)(4,1)}, u32[]{:S(2)}) copy-start(pred[384]{0:T(512)(128)(4,1)} %dynamic_slice.7) | copy-start | bytes 1156
Sparse Core Ops, SparseCore 0:
  9.9 81.6 all-gather.2
  199.8 44.9 reduce-scatter.3
  247.3 124.6 all-gather.4
